TPU v7x, 32 devices: a whole 2x2x4 slice. The times are simulated.
32 devices in a mesh: groups: 2 (over y), patch: 4 (over z), fsdp: 2 (over x), cfg: 2 (over core).
Axes of the slice: x: 2, y: 2, z: 4, core: 2. Of those that a mesh axis runs over, the one named last changes fastest.
Arguments:
- hidden_states: bfloat16 [4, 1536, 5120], P(('groups', 'cfg'), 'patch', 'fsdp'), parts along dimension 0, may hold values from -6 to 6
- queries: bfloat16 [4, 1536, 2560], P(('groups', 'cfg'), 'patch', 'fsdp'), parts along dimension 0, may hold values from -8 to 8
- fresh_kv: bfloat16 [4, 2, 1536, 2560], P(('groups', 'cfg'), None, 'patch', 'fsdp'), parts along dimension 0, may hold values from -8 to 8
- stale_kv: bfloat16 [4, 2, 1536, 2560], P(('groups', 'cfg'), None, 'patch', 'fsdp'), parts along dimension 0, may hold values from -8 to 8
- out_weight: bfloat16 [2560, 5120], P('fsdp'), may hold values from -0.125 to 0.125
- gate_table: float32 [50, 5120], P(None, 'fsdp'), may hold values from -4 to 4
- timestep: int32 [2], P('groups'), parts along dimension 0, may hold values from 0 to 49
Outputs:
- block_out: bfloat16 [4, 1536, 5120], P(('groups', 'cfg'), 'patch', 'fsdp'), parts along dimension 0
There are 2 independent parts, one for each index of `groups`. A program takes and returns all parts, laid end to end along the dimension named above; an argument that names none is the same for every part. Nothing has to cross between parts.
All inputs are finite; a program needn't handle non-finite values.
Results may differ from a plain program's by a relative error of at most 0.0065.
Values may be sent and summed in bfloat16 or wider, within the bound.
A program may use at most 128 MiB of HBM per device.

v0:
```python
import jax
import jax.numpy as jnp
from jax import lax
from jax.sharding import PartitionSpec as P

HEAD = 128


def dense_head(query_head, key_head, value_head):
    scores = jnp.einsum(
        "qd,kd->qk", query_head, key_head, preferred_element_type=jnp.float32
    ) * HEAD ** (-0.5)
    peak = jnp.max(scores, axis=-1, keepdims=True)
    weights = jnp.exp(scores - peak)
    total = jnp.sum(weights, axis=-1, keepdims=True)
    probs = weights.astype(jnp.bfloat16)
    return jnp.dot(probs, value_head, preferred_element_type=jnp.float32) / total


def local(hidden_states, queries, fresh_kv, stale_kv, out_weight, gate_table, timestep):
    rows_here = queries.shape[1]
    width = queries.shape[2]
    heads_here = width // HEAD
    query_local = queries[0]
    own_start = lax.axis_index("patch") * rows_here
    head_ids = jnp.arange(heads_here, dtype=jnp.int32)
    gathered = lax.all_gather(stale_kv, "patch", axis=2, tiled=True)[0]
    merged = lax.dynamic_update_slice_in_dim(gathered, fresh_kv[0], own_start, 1)

    def one_head(head):
        offset = head * HEAD
        query_head = lax.dynamic_slice_in_dim(query_local, offset, HEAD, 1)
        key_head = lax.dynamic_slice_in_dim(merged[0], offset, HEAD, 1)
        value_head = lax.dynamic_slice_in_dim(merged[1], offset, HEAD, 1)
        return dense_head(query_head, key_head, value_head)

    stacked = lax.map(one_head, head_ids)
    attention = jnp.transpose(stacked, (1, 0, 2)).reshape(rows_here, width).astype(jnp.bfloat16)
    blocks = lax.axis_size("fsdp")
    all_heads = lax.all_gather(attention, "fsdp", axis=1, tiled=True)
    columns = lax.all_to_all(out_weight, "fsdp", split_axis=1, concat_axis=0, tiled=True)
    heads_blocked = all_heads.reshape(rows_here, blocks, width)
    columns_blocked = columns.reshape(blocks, width, columns.shape[1])
    terms = jnp.einsum(
        "rfk,fkd->frd", heads_blocked, columns_blocked, preferred_element_type=jnp.float32
    )
    rounded = lax.optimization_barrier(terms.astype(jnp.bfloat16)).astype(jnp.float32)
    projected = jnp.sum(rounded, axis=0)
    gate_row = lax.dynamic_index_in_dim(gate_table, timestep[0], 0, keepdims=False)
    block_out = hidden_states[0].astype(jnp.float32) + gate_row[None, :] * projected
    return block_out.astype(jnp.bfloat16)[None]


def solution(mesh):
    in_specs = (
        P(("groups", "cfg"), "patch", "fsdp"),
        P(("groups", "cfg"), "patch", "fsdp"),
        P(("groups", "cfg"), None, "patch", "fsdp"),
        P(("groups", "cfg"), None, "patch", "fsdp"),
        P("fsdp", None),
        P(None, "fsdp"),
        P("groups"),
    )
    out_specs = P(("groups", "cfg"), "patch", "fsdp")
    return jax.shard_map(local, mesh=mesh, in_specs=in_specs, out_specs=out_specs, check_vma=False)
```

profile of v0, /device:TPU:0, one launch (start us, length us, event | category | flops | bytes accessed | tf_op | source)
XLA Modules:
  0.0 279.6 jit_solution(16755228770092753722)
XLA Ops:
  6.5 0.7 all-gather.3.cloned.1.call-update
  7.3 18.0 %copy.9 = bf16[1280,5120]{0,1:T(8,128)(2,1)} copy(bf16[1280,5120]{1,0:T(8,128)(2,1)} %param.13) | data formatting | bytes 26214400 | tf_op args[4]
  25.3 17.7 %copy.10 = bf16[1280,2,2560]{2,0,1:T(8,128)(2,1)} copy(bf16[1280,2,2560]{0,2,1:T(8,128)(2,1)} %bitcast.45) | data formatting | bytes 26214400 | tf_op jit(solution)/shard_map/all_to_all | solution.py:41
  43.0 8.6 %all-to-all-start = ((bf16[1280,2,2560]{2,0,1:T(8,128)(2,1)}), bf16[1280,2,2560]{2,0,1:T(8,128)(2,1)}, u32[]{:S(2)}, u32[]{:S(2)}) async-start(bf16[1280,2,2560]{2,0,1:T(8,128)(2,1)} %copy.10), calls=%async_computation | async-start | bytes 26214400 | tf_op jit(solution)/shard_map/all_to_all | solution.py:41
  51.7 101.0 %all-gather.3.cloned.1.call-done = bf16[1,2,1536,1280]{3,2,1,0:T(8,128)(2,1)} async-done(((bf16[1,2,384,1280]{3,2,1,0:T(8,128)(2,1)}), bf16[1,2,1536,1280]{3,2,1,0:T(8,128)(2,1)}) %all-gather.3.cloned.1.call-update) | async-done | bytes 7864336 | tf_op jit(solution)/shard_map/all_gather | solution.py:27
  152.7 1.4 bitcast_dynamic-update-slice_fusion
  154.1 75.2 %while.10 = (s32[]{:T(128)}, bf16[10,384,128]{1,2,0:T(8,128)(2,1)S(1)}, s32[10]{0:T(128)S(1)}, bf16[384,1280]{1,0:T(8,128)(2,1)}, bf16[2,1536,1280]{2,1,0:T(8,12...) while((s32[]{:T(128)}, bf16[10,384,128]{1,2,0:T(8,128)(2,1)S(1)}, s32[10]{0:T(128)S(1)}, ...), condition=%wide.region_3.4_spmd, body=%wide.region_0.3_spmd.sunk | while | flops 305626368 | bytes 24192672 | solution.py:37
  154.1 0.6 dynamic_slice.44
  155.4 3.6 %fusion.36 = (bf16[1,1536,1280]{2,1,0:T(8,128)(2,1)S(1)}, bf16[1,1536,1280]{2,1,0:T(8,128)(2,1)S(1)}) fusion(bf16[2,1536,1280]{2,1,0:T(8,128)(2,1)} %get-tuple-element.108), kind=kLoop, calls=%fused_computation.25.clone.1 | loop fusion | bytes 15728640 | tf_op jit(solution)/shard_map/while/body/eval_jaxpr/slice | solution.py:34
  159.0 1.5 fusion.37
  161.6 0.6 dynamic_slice.44
  162.9 3.6 %fusion.36 = (bf16[1,1536,1280]{2,1,0:T(8,128)(2,1)S(1)}, bf16[1,1536,1280]{2,1,0:T(8,128)(2,1)S(1)}) fusion(bf16[2,1536,1280]{2,1,0:T(8,128)(2,1)} %get-tuple-element.108), kind=kLoop, calls=%fused_computation.25.clone.1 | loop fusion | bytes 15728640 | tf_op jit(solution)/shard_map/while/body/eval_jaxpr/slice | solution.py:34
  166.5 1.5 fusion.37
  169.1 0.6 dynamic_slice.44
  170.4 3.6 %fusion.36 = (bf16[1,1536,1280]{2,1,0:T(8,128)(2,1)S(1)}, bf16[1,1536,1280]{2,1,0:T(8,128)(2,1)S(1)}) fusion(bf16[2,1536,1280]{2,1,0:T(8,128)(2,1)} %get-tuple-element.108), kind=kLoop, calls=%fused_computation.25.clone.1 | loop fusion | bytes 15728640 | tf_op jit(solution)/shard_map/while/body/eval_jaxpr/slice | solution.py:34
  174.0 1.5 fusion.37
  175.9 0.5 fusion.39
  176.7 0.6 dynamic_slice.44
  177.9 3.6 %fusion.36 = (bf16[1,1536,1280]{2,1,0:T(8,128)(2,1)S(1)}, bf16[1,1536,1280]{2,1,0:T(8,128)(2,1)S(1)}) fusion(bf16[2,1536,1280]{2,1,0:T(8,128)(2,1)} %get-tuple-element.108), kind=kLoop, calls=%fused_computation.25.clone.1 | loop fusion | bytes 15728640 | tf_op jit(solution)/shard_map/while/body/eval_jaxpr/slice | solution.py:34
  181.5 1.5 fusion.37
  183.5 0.5 fusion.39
  184.2 0.6 dynamic_slice.44
  185.5 3.6 %fusion.36 = (bf16[1,1536,1280]{2,1,0:T(8,128)(2,1)S(1)}, bf16[1,1536,1280]{2,1,0:T(8,128)(2,1)S(1)}) fusion(bf16[2,1536,1280]{2,1,0:T(8,128)(2,1)} %get-tuple-element.108), kind=kLoop, calls=%fused_computation.25.clone.1 | loop fusion | bytes 15728640 | tf_op jit(solution)/shard_map/while/body/eval_jaxpr/slice | solution.py:34
  189.1 1.5 fusion.37
  191.0 0.6 fusion.39
  191.7 0.6 dynamic_slice.44
  193.0 3.6 %fusion.36 = (bf16[1,1536,1280]{2,1,0:T(8,128)(2,1)S(1)}, bf16[1,1536,1280]{2,1,0:T(8,128)(2,1)S(1)}) fusion(bf16[2,1536,1280]{2,1,0:T(8,128)(2,1)} %get-tuple-element.108), kind=kLoop, calls=%fused_computation.25.clone.1 | loop fusion | bytes 15728640 | tf_op jit(solution)/shard_map/while/body/eval_jaxpr/slice | solution.py:34
  196.6 1.5 fusion.37
  198.5 0.6 fusion.39
  199.2 0.6 dynamic_slice.44
  200.5 3.6 %fusion.36 = (bf16[1,1536,1280]{2,1,0:T(8,128)(2,1)S(1)}, bf16[1,1536,1280]{2,1,0:T(8,128)(2,1)S(1)}) fusion(bf16[2,1536,1280]{2,1,0:T(8,128)(2,1)} %get-tuple-element.108), kind=kLoop, calls=%fused_computation.25.clone.1 | loop fusion | bytes 15728640 | tf_op jit(solution)/shard_map/while/body/eval_jaxpr/slice | solution.py:34
  204.1 1.5 fusion.37
  206.8 0.6 dynamic_slice.44
  208.0 3.6 %fusion.36 = (bf16[1,1536,1280]{2,1,0:T(8,128)(2,1)S(1)}, bf16[1,1536,1280]{2,1,0:T(8,128)(2,1)S(1)}) fusion(bf16[2,1536,1280]{2,1,0:T(8,128)(2,1)} %get-tuple-element.108), kind=kLoop, calls=%fused_computation.25.clone.1 | loop fusion | bytes 15728640 | tf_op jit(solution)/shard_map/while/body/eval_jaxpr/slice | solution.py:34
  211.6 1.5 fusion.37
  213.6 0.5 fusion.39
  214.3 0.6 dynamic_slice.44
  215.6 3.6 %fusion.36 = (bf16[1,1536,1280]{2,1,0:T(8,128)(2,1)S(1)}, bf16[1,1536,1280]{2,1,0:T(8,128)(2,1)S(1)}) fusion(bf16[2,1536,1280]{2,1,0:T(8,128)(2,1)} %get-tuple-element.108), kind=kLoop, calls=%fused_computation.25.clone.1 | loop fusion | bytes 15728640 | tf_op jit(solution)/shard_map/while/body/eval_jaxpr/slice | solution.py:34
  219.2 1.5 fusion.37
  221.8 0.6 dynamic_slice.44
  223.1 3.6 %fusion.36 = (bf16[1,1536,1280]{2,1,0:T(8,128)(2,1)S(1)}, bf16[1,1536,1280]{2,1,0:T(8,128)(2,1)S(1)}) fusion(bf16[2,1536,1280]{2,1,0:T(8,128)(2,1)} %get-tuple-element.108), kind=kLoop, calls=%fused_computation.25.clone.1 | loop fusion | bytes 15728640 | tf_op jit(solution)/shard_map/while/body/eval_jaxpr/slice | solution.py:34
  226.7 1.5 fusion.37
  229.3 0.9 copy-done.3
  231.0 29.3 %all-gather.5.cloned.1.call-done = bf16[384,2560]{0,1:T(8,128)(2,1)} async-done(((bf16[384,1280]{0,1:T(8,128)(2,1)}), bf16[384,2560]{0,1:T(8,128)(2,1)}) %all-gather.5.cloned.1.call-update) | async-done | bytes 1966096 | tf_op jit(solution)/shard_map/all_gather | solution.py:40
  260.3 9.1 %fusion.20 = bf16[2,384,2560]{2,1,0:T(8,128)(2,1)S(1)} fusion(bf16[384,2,1280]{0,2,1:T(8,128)(2,1)} %bitcast.48, bf16[1280,2,2560]{2,0,1:T(8,128)(2,1)} %all-to-all-done), kind=kOutput, calls=%fused_computation.19 | convolution fusion | flops 5035130880 | bytes 19005440 | tf_op jit(solution)/shard_map/rfk,fkd->frd/dot_general | solution.py:44
  269.4 0.7 convert_reduce_fusion
  270.1 0.8 copy-done.2
  270.9 1.8 fusion.24
  (48 shorter events, 9.0 us)
Async XLA Ops:
  6.5 224.4 %copy-start = (f32[50,2560]{1,0:T(8,128)S(1)}, f32[50,2560]{1,0:T(8,128)}, u32[]{:S(2)}) copy-start(f32[50,2560]{1,0:T(8,128)} %param.14) | copy-start | bytes 1536004
  6.5 146.2 %all-gather.3.cloned.1.call-start = ((), (), s32[]{:S(2)}) async-start(), calls=%async_computation.1 | async-start | bytes 9830400 | tf_op jit(solution)/shard_map/all_gather | solution.py:27
  43.0 109.7 %copy-start.1 = (bf16[1,2,384,1280]{3,2,1,0:T(8,128)(2,1)S(1)}, bf16[1,2,384,1280]{3,2,1,0:T(8,128)(2,1)}, u32[]{:S(2)}) copy-start(bf16[1,2,384,1280]{3,2,1,0:T(8,128)(2,1)} %param.11) | copy-start | bytes 5898244
  43.0 188.0 %all-to-all-start = ((bf16[1280,2,2560]{2,0,1:T(8,128)(2,1)}), bf16[1280,2,2560]{2,0,1:T(8,128)(2,1)}, u32[]{:S(2)}, u32[]{:S(2)}) async-start(bf16[1280,2,2560]{2,0,1:T(8,128)(2,1)} %copy.10), calls=%async_computation | async-start | bytes 26214400 | tf_op jit(solution)/shard_map/all_to_all | solution.py:41
  51.7 208.6 %all-gather.5.cloned.1.call-start = ((), (), s32[]{:S(2)}) async-start(), calls=%async_computation.2 | async-start | bytes 2949120 | tf_op jit(solution)/shard_map/all_gather | solution.py:40
  229.3 0.9 copy-start.3
  269.4 1.5 copy-start.2
Sparse Core Ops, SparseCore 0:
  8.9 143.7 all-gather.2
  230.4 29.8 all-gather.4
where the time goes:
time: 281 us; the launch traced here: 280 us
  waiting for transfers between devices  131 us (47%)
  local copies, waits for them, and re-layouts  82.8 us (29%)
  matrix products  29.1 us (10%)
  between operations  14.1 us (5%)
  starting transfers between devices  8.67 us (3%)
  other arithmetic  7.26 us (3%)
  loops' own time  6.68 us (2%)
    all_gather x1, waiting for transfers between devices, local(): gathered = lax.all_gather(stale_kv, 'patch', axis=2, tiled=True)[0]  101 us
    slice x10, local copies, waits for them, and re-layouts, one_head(): value_head = lax.dynamic_slice_in_dim(merged[1], offset, HEAD, 1)  36 us
    all_gather x1, waiting for transfers between devices, local(): all_heads = lax.all_gather(attention, 'fsdp', axis=1, tiled=True)  29.3 us
    unnamed x9, local copies, waits for them, and re-layouts  19.8 us
    all_to_all x1, local copies, waits for them, and re-layouts, local(): lax.all_to_all(out_weight, 'fsdp', split_axis=1, concat_axis=0, tiled=True)  17.7 us
    dot_general x10, matrix products, dense_head(): jnp.einsum('qd,kd->qk', query_head, key_head, preferred_element_type=jnp....  14.5 us
    dot_general x1, matrix products, local(): jnp.einsum('rfk,fkd->frd', heads_blocked, columns_blocked, preferred_elem...  9.1 us
    all_to_all x1, starting transfers between devices, local(): lax.all_to_all(out_weight, 'fsdp', split_axis=1, concat_axis=0, tiled=True)  8.62 us
  transfers between devices with their start and end apart: 3, of which 2 were waited for; matrix products, arithmetic and copies ran while one was open for 38% of the time, Pallas kernels for 0%

commit v1 on v0

--- a/solution.py
+++ b/solution.py
@@ -1,6 +1,11 @@
+import functools
+import math
+
 import jax
 import jax.numpy as jnp
 from jax import lax
+from jax.experimental import pallas as pl
+from jax.experimental.pallas import tpu as pltpu
 from jax.sharding import PartitionSpec as P
 
 HEAD = 128
@@ -51,6 +56,350 @@
     return block_out.astype(jnp.bfloat16)[None]
 
 
+MESH = pl.DeviceIdType.MESH
+LEAD = 3
+
+
+def attend_head(q_ref, q_cols, k_ref, v_ref, kv_cols, o_ref, o_cols):
+    rows = q_ref.shape[0]
+    tile = 128
+    factor = HEAD ** (-0.5) * math.log2(math.e)
+    keys = k_ref[:, kv_cols]
+    values = v_ref[:, kv_cols]
+    for start in range(0, rows, tile):
+        part = slice(start, start + tile)
+        scores = lax.dot_general(
+            q_ref[part, q_cols], keys, (((1,), (1,)), ((), ())), preferred_element_type=jnp.float32
+        )
+        peak = jnp.max(scores, axis=-1, keepdims=True)
+        weights = jnp.exp2((scores - peak) * factor)
+        total = jnp.sum(weights, axis=-1, keepdims=True)
+        summed = jnp.dot(weights.astype(jnp.bfloat16), values, preferred_element_type=jnp.float32)
+        o_ref[part, o_cols] = (summed / total).astype(jnp.bfloat16)
+
+
+def fused_kernel(
+    far_heads, hidden_ref, q_hbm, fresh_ref, stale_ref, w_ref, gate_ref, out_ref,
+    kv, q, helped_kv, helped_q, helped_out, att, att_peer, w_own, w_peer, hidden,
+    local_sem, kv_send, kv_recv, edge_send, edge_recv, res_send, res_recv,
+    att_send, att_recv, w_send, w_recv,
+):
+    rows, width = q.shape
+    heads = width // HEAD
+    last = lax.axis_size("patch") - 1
+    near = heads - far_heads
+    columns = w_own.shape[1]
+    z = lax.axis_index("patch")
+    f = lax.axis_index("fsdp")
+    g = lax.axis_index("groups")
+    c = lax.axis_index("cfg")
+    is_edge = (z == 0) | (z == last)
+    inner = jnp.logical_not(is_edge)
+    inward = jnp.where(z == 0, 1, jnp.where(z == last, z - 1, z))
+    edge = jnp.where(z <= 1, 0, last)
+    edge_to = jnp.where(is_edge, jnp.where(z == 0, 1, last - 1), edge)
+
+    def cols(t):
+        return pl.ds(pl.multiple_of(t * HEAD, HEAD), HEAD)
+
+    def span(p):
+        return pl.ds(pl.multiple_of(p * rows, rows), rows)
+
+    def remote(src, dst, send, recv, axis, index):
+        return pltpu.make_async_remote_copy(
+            src_ref=src, dst_ref=dst, send_sem=send, recv_sem=recv,
+            device_id={axis: index}, device_id_type=MESH,
+        )
+
+    barrier = pltpu.get_barrier_semaphore()
+    for axis in ("fsdp", "groups", "cfg"):
+        pl.semaphore_signal(barrier, 1, device_id={axis: 1 - lax.axis_index(axis)}, device_id_type=MESH)
+
+    @pl.when(z > 0)
+    def _():
+        pl.semaphore_signal(barrier, 1, device_id={"patch": z - 1}, device_id_type=MESH)
+
+    @pl.when(z < last)
+    def _():
+        pl.semaphore_signal(barrier, 1, device_id={"patch": z + 1}, device_id_type=MESH)
+
+    @pl.when(is_edge)
+    def _():
+        pl.semaphore_wait(barrier, 4)
+
+    @pl.when(inner)
+    def _():
+        pl.semaphore_wait(barrier, 5)
+
+    def kv_copy(way, hop, t):
+        step = 1 if way == 0 else -1
+        source = z - step * hop
+        here = kv.at[:, span(source), cols(t)]
+        src = stale_ref.at[0, :, :, cols(t)] if hop == 0 else here
+        return remote(src, here, kv_send.at[way, hop, t], kv_recv.at[source, t], "patch", z + step)
+
+    def kv_arrival(way, hop, t):
+        step = 1 if way == 0 else -1
+        source = z - step * hop
+        here = kv.at[:, span(source), cols(t)]
+        return remote(here, here, kv_send.at[way, 0, t], kv_recv.at[source, t], "patch", z - step)
+
+    def source_there(way, hop):
+        return z - hop >= 0 if way == 0 else z + hop <= last
+
+    def may_send(way, t):
+        if way == 0:
+            return (z + 1 <= last) & ((z + 1 < last) | (t < near))
+        return (z >= 1) & ((z - 1 > 0) | (t < near))
+
+    def does_send(way, hop, t):
+        return source_there(way, hop) & may_send(way, t)
+
+    def does_receive(way, hop, t):
+        return source_there(way, hop) & (inner | (t < near))
+
+    def send_own(t):
+        for way in (0, 1):
+            @pl.when(does_send(way, 0, t))
+            def _():
+                kv_copy(way, 0, t).start()
+
+    def take(hop, t):
+        for way in (0, 1):
+            @pl.when(does_receive(way, hop, t))
+            def _():
+                kv_arrival(way, hop, t).wait_recv()
+
+            if hop < 3:
+                @pl.when(does_send(way, hop, t))
+                def _():
+                    kv_copy(way, hop, t).start()
+
+    def edge_q(i):
+        return remote(
+            q_hbm.at[0, :, cols(near + i)], helped_q.at[:, cols(i)],
+            edge_send.at[0, i], edge_recv.at[0, i], "patch", edge_to)
+
+    def edge_kv(i):
+        return remote(
+            fresh_ref.at[0, :, :, cols(near + i)],
+            helped_kv.at[:, span(z), cols(i)],
+            edge_send.at[1, i], edge_recv.at[1, i], "patch", edge_to)
+
+    def edge_kv_arrival(i):
+        here = helped_kv.at[:, span(edge), cols(i)]
+        return remote(here, here, edge_send.at[1, i], edge_recv.at[1, i], "patch", edge_to)
+
+    def result_copy(i):
+        return remote(
+            helped_out.at[:, cols(i)], att.at[:, cols(near + i)],
+            res_send.at[i], res_recv.at[i], "patch", edge_to)
+
+    def att_copy(t):
+        return remote(att.at[:, cols(t)], att_peer.at[:, cols(t)], att_send.at[t], att_recv.at[t], "fsdp", 1 - f)
+
+    quarter = w_peer.shape[0] // 4
+
+    def w_rows(gi, ci):
+        return pl.ds(pl.multiple_of((gi * 2 + ci) * quarter, quarter), quarter)
+
+    def w_x():
+        there = pl.ds(pl.multiple_of((1 - f) * columns, columns), columns)
+        return remote(
+            w_ref.at[w_rows(g, c), there], w_peer.at[w_rows(g, c), :],
+            w_send.at[0], w_recv.at[0], "fsdp", 1 - f)
+
+    def w_y():
+        here = w_peer.at[w_rows(g, c), :]
+        return remote(here, here, w_send.at[1], w_recv.at[1], "groups", 1 - g)
+
+    def w_core(k):
+        here = w_peer.at[w_rows(g if k == 0 else 1 - g, c), :]
+        return remote(here, here, w_send.at[2 + k], w_recv.at[2 + k], "cfg", 1 - c)
+
+    @pl.when(is_edge)
+    def _():
+        @pl.loop(0, heads)
+        def _(t):
+            send_own(t)
+
+            @pl.when(t >= near)
+            def _():
+                edge_q(t - near).start()
+                edge_kv(t - near).start()
+
+    @pl.when(inner)
+    def _():
+        @pl.loop(0, LEAD)
+        def _(t):
+            send_own(t)
+
+    w_x().start()
+    q_in = pltpu.make_async_copy(q_hbm.at[0], q, local_sem.at[0])
+    fresh_in = pltpu.make_async_copy(fresh_ref.at[0], kv.at[:, span(z), :], local_sem.at[1])
+    hidden_in = pltpu.make_async_copy(hidden_ref.at[0], hidden, local_sem.at[2])
+    w_in = pltpu.make_async_copy(
+        w_ref.at[:, pl.ds(pl.multiple_of(f * columns, columns), columns)], w_own, local_sem.at[3])
+    stale_in = pltpu.make_async_copy(
+        stale_ref.at[0, :, :, pl.ds(near * HEAD, far_heads * HEAD)],
+        helped_kv.at[:, span(z), :], local_sem.at[4])
+    q_in.start()
+    fresh_in.start()
+
+    @pl.when(inner)
+    def _():
+        stale_in.start()
+
+    hidden_in.start()
+    w_in.start()
+    q_in.wait()
+    fresh_in.wait()
+
+    @pl.when(inner)
+    def _():
+        stale_in.wait()
+
+    take(1, 0)
+    x_step = jnp.where(is_edge, 2, 4)
+    y_step = jnp.where(is_edge, near, heads - 1)
+
+    @pl.loop(0, heads)
+    def _(t):
+        @pl.when(inner & (t + LEAD < heads))
+        def _():
+            send_own(t + LEAD)
+
+        @pl.when(t + 1 < heads)
+        def _():
+            take(1, t + 1)
+
+        take(2, t)
+        take(3, t)
+
+        @pl.when(t == x_step)
+        def _():
+            w_x().wait_recv()
+            w_y().start()
+            w_core(0).start()
+
+        @pl.when(t == y_step)
+        def _():
+            w_y().wait_recv()
+            w_core(1).start()
+
+        @pl.when(inner & (t >= near))
+        def _():
+            i = t - near
+            edge_q(i).wait_recv()
+            edge_kv_arrival(i).wait_recv()
+            for p in range(4):
+                @pl.when((z != p) & (edge != p))
+                def _():
+                    part = slice(p * rows, (p + 1) * rows)
+                    helped_kv[:, part, cols(i)] = kv[:, part, cols(t)]
+            attend_head(helped_q, cols(i), helped_kv.at[0], helped_kv.at[1], cols(i), helped_out, cols(i))
+            result_copy(i).start()
+
+        @pl.when(inner | (t < near))
+        def _():
+            attend_head(q, cols(t), kv.at[0], kv.at[1], cols(t), att, cols(t))
+
+        @pl.when(is_edge & (t >= near))
+        def _():
+            result_copy(t - near).wait_recv()
+
+        att_copy(t).start()
+
+    w_in.wait()
+    hidden_in.wait()
+    w_core(0).wait_recv()
+    w_core(1).wait_recv()
+
+    @pl.loop(0, heads)
+    def _(t):
+        att_copy(t).wait_recv()
+
+    step = 512
+
+    @pl.loop(0, columns // step)
+    def _(n):
+        part = pl.ds(pl.multiple_of(n * step, step), step)
+        mine = jnp.dot(att[...], w_own[:, part], preferred_element_type=jnp.float32)
+        other = jnp.dot(att_peer[...], w_peer[:, part], preferred_element_type=jnp.float32)
+        projected = mine.astype(jnp.bfloat16).astype(jnp.float32) + other.astype(jnp.bfloat16).astype(jnp.float32)
+        moved = hidden[:, part].astype(jnp.float32) + gate_ref[:, part] * projected
+        out_ref[:, part] = moved.astype(jnp.bfloat16)
+
+    w_x().wait_send()
+    w_y().wait_send()
+    w_core(0).wait_send()
+    w_core(1).wait_send()
+
+    @pl.loop(0, heads)
+    def _(t):
+        att_copy(t).wait_send()
+        for way in (0, 1):
+            for hop in (0, 1, 2):
+                @pl.when(does_send(way, hop, t))
+                def _():
+                    kv_copy(way, hop, t).wait_send()
+
+    @pl.loop(0, far_heads)
+    def _(i):
+        @pl.when(is_edge)
+        def _():
+            edge_q(i).wait_send()
+            edge_kv(i).wait_send()
+
+        @pl.when(inner)
+        def _():
+            result_copy(i).wait_send()
+
+
+def fused_local(hidden_states, queries, fresh_kv, stale_kv, out_weight, gate_table, timestep):
+    rows, width = queries.shape[1:]
+    heads = width // HEAD
+    tokens = rows * lax.axis_size("patch")
+    columns = hidden_states.shape[2]
+    far_heads = (2 * heads) // 5
+    gate_row = lax.dynamic_index_in_dim(gate_table, timestep[0], 0, keepdims=True)
+    bf16 = jnp.bfloat16
+    hbm = pl.BlockSpec(memory_space=pl.ANY)
+    dma = pltpu.SemaphoreType.DMA
+    out = pl.pallas_call(
+        functools.partial(fused_kernel, far_heads),
+        out_shape=jax.ShapeDtypeStruct((rows, columns), bf16),
+        in_specs=[hbm] * 5 + [pl.BlockSpec(memory_space=pltpu.VMEM)],
+        out_specs=pl.BlockSpec(memory_space=pltpu.VMEM),
+        scratch_shapes=[
+            pltpu.VMEM((2, tokens, width), bf16),
+            pltpu.VMEM((rows, width), bf16),
+            pltpu.VMEM((2, tokens, far_heads * HEAD), bf16),
+            pltpu.VMEM((rows, far_heads * HEAD), bf16),
+            pltpu.VMEM((rows, far_heads * HEAD), bf16),
+            pltpu.VMEM((rows, width), bf16),
+            pltpu.VMEM((rows, width), bf16),
+            pltpu.VMEM((width, columns), bf16),
+            pltpu.VMEM((width, columns), bf16),
+            pltpu.VMEM((rows, columns), bf16),
+            dma((5,)),
+            dma((2, 3, heads)),
+            dma((4, heads)),
+            dma((2, far_heads)),
+            dma((2, far_heads)),
+            dma((far_heads,)),
+            dma((far_heads,)),
+            dma((heads,)),
+            dma((heads,)),
+            dma((4,)),
+            dma((4,)),
+        ],
+        compiler_params=pltpu.CompilerParams(
+            collective_id=0, has_side_effects=True, vmem_limit_bytes=56 << 20),
+    )(hidden_states, queries, fresh_kv, stale_kv, out_weight, gate_row)
+    return out[None]
+
+
 def solution(mesh):
     in_specs = (
         P(("groups", "cfg"), "patch", "fsdp"),
@@ -62,4 +411,7 @@
         P("groups"),
     )
     out_specs = P(("groups", "cfg"), "patch", "fsdp")
-    return jax.shard_map(local, mesh=mesh, in_specs=in_specs, out_specs=out_specs, check_vma=False)
+    body = local
+    if mesh.shape["patch"] == 4 and mesh.shape["fsdp"] == 2 and mesh.shape["groups"] == 2 and mesh.shape["cfg"] == 2:
+        body = fused_local
+    return jax.shard_map(body, mesh=mesh, in_specs=in_specs, out_specs=out_specs, check_vma=False)

time: 281 us -> 119 us (0.42)
  waiting for transfers between devices: 131 us -> 0 us
  Pallas kernels: 0 us -> 114 us
  local copies, waits for them, and re-layouts: 82.8 us -> 3.91 us
  matrix products: 29.1 us -> 0 us
  between operations: 14.1 us -> 0.73 us
  starting transfers between devices: 8.67 us -> 0 us
  other arithmetic: 7.26 us -> 0 us
  loops' own time: 6.68 us -> 0 us
    all_gather x2 -> x0, waiting for transfers between devices: 130 us -> none  [the longest x1 101 us: local(): gathered = lax.all_gather(stale_kv, 'patch', axis=2, tiled=True)[0]]
    pallas_call x0 -> x1, Pallas kernels: none -> 114 us  [fused_local(): pl.pallas_call(functools.partial(fused_kernel, far_heads), out_shape=jax....]
    slice x10 -> x0, local copies, waits for them, and re-layouts: 36 us -> none  [one_head(): value_head = lax.dynamic_slice_in_dim(merged[1], offset, HEAD, 1)]
    dot_general x21 -> x0, matrix products: 29.1 us -> none  [the longest x10 14.5 us: dense_head(): jnp.einsum('qd,kd->qk', query_head, key_head, preferred_element_type=jnp....]
    all_to_all x1 -> x0, local copies, waits for them, and re-layouts: 17.7 us -> none  [local(): lax.all_to_all(out_weight, 'fsdp', split_axis=1, concat_axis=0, tiled=True)]
    unnamed x9 -> x3, local copies, waits for them, and re-layouts: 19.8 us -> 3.3 us
    all_to_all x1 -> x0, starting transfers between devices: 8.62 us -> none  [local(): lax.all_to_all(out_weight, 'fsdp', split_axis=1, concat_axis=0, tiled=True)]
    another operation x1 -> x0, loops' own time: 6.68 us -> none  [local(): stacked = lax.map(one_head, head_ids)]
  transfers between devices with their start and end apart: 3 -> 0, of which waited for: 2 -> 0; matrix products, arithmetic and copies ran while one was open for 38% -> 0% of each run, Pallas kernels for 0% -> 0%
where the time goes in v1:
time: 119 us
  Pallas kernels  114 us (96%)
  local copies, waits for them, and re-layouts  3.91 us (3%)
    pallas_call x1, Pallas kernels, fused_local(): pl.pallas_call(functools.partial(fused_kernel, far_heads), out_shape=jax....  114 us
    unnamed x3, local copies, waits for them, and re-layouts  3.3 us

profile of v1, /device:TPU:0, one launch (start us, length us, event | category | flops | bytes accessed | tf_op | source)
XLA Modules:
  0.0 119.0 jit_solution(10390562768566273947)
XLA Ops:
  0.0 0.0 copy-start
  0.7 0.4 copy-done
  1.1 0.6 constant_dynamic-slice_fusion.gate_ref
  1.7 114.4 %shard_map.73 = bf16[384,2560]{1,0:T(8,128)(2,1)} custom-call(bf16[1,384,2560]{2,1,0:T(8,128)(2,1)} %hidden_ref.1, bf16[1,384,1280]{2,1,0:T(8,128)(2,1)} %q_hbm.1, bf16[1,2,384,1280]{3,2,1,0:T(8,128)(2,1)} %fresh_ref.1, bf16[1,2,384,1280]{3,2,1,0:T(8,128)(2,1)} %stale_ref.1, bf16[1280,5120]{1,0:T(8,128)(2,1)} %w_ref.1, ...), custom_call_target="tpu_custom_call" | custom-call | tf_op jit(solution)/shard_map/pallas_call | solution.py:369
  116.1 2.9 %copy.10 = bf16[1,384,2560]{2,1,0:T(8,128)(2,1)} copy(bf16[1,384,2560]{2,1,0:T(8,128)(2,1)} %bitcast.5) | data formatting | bytes 3932160
Async XLA Ops:
  0.0 1.1 copy-start

commit v2 on v1

--- a/solution.py
+++ b/solution.py
@@ -79,8 +79,8 @@
 
 
 def fused_kernel(
-    far_heads, hidden_ref, q_hbm, fresh_ref, stale_ref, w_ref, gate_ref, out_ref,
-    kv, q, helped_kv, helped_q, helped_out, att, att_peer, w_own, w_peer, hidden,
+    far_heads, hidden_ref, q_hbm, fresh_ref, stale_ref, w_ref, gate_ref, when_ref, out_ref,
+    kv, q, helped_kv, helped_q, helped_out, att, att_peer, w_own, w_peer, hidden, gates, total,
     local_sem, kv_send, kv_recv, edge_send, edge_recv, res_send, res_recv,
     att_send, att_recv, w_send, w_recv,
 ):
@@ -198,24 +198,24 @@
     def att_copy(t):
         return remote(att.at[:, cols(t)], att_peer.at[:, cols(t)], att_send.at[t], att_recv.at[t], "fsdp", 1 - f)
 
-    quarter = w_peer.shape[0] // 4
-
-    def w_rows(gi, ci):
-        return pl.ds(pl.multiple_of((gi * 2 + ci) * quarter, quarter), quarter)
-
-    def w_x():
+    piece = w_peer.shape[0] // 16
+
+    def w_rows(gi, ci, k):
+        return pl.ds(pl.multiple_of(((gi * 2 + ci) * 4 + k) * piece, piece), piece)
+
+    def w_x(k):
         there = pl.ds(pl.multiple_of((1 - f) * columns, columns), columns)
         return remote(
-            w_ref.at[w_rows(g, c), there], w_peer.at[w_rows(g, c), :],
-            w_send.at[0], w_recv.at[0], "fsdp", 1 - f)
-
-    def w_y():
-        here = w_peer.at[w_rows(g, c), :]
-        return remote(here, here, w_send.at[1], w_recv.at[1], "groups", 1 - g)
-
-    def w_core(k):
-        here = w_peer.at[w_rows(g if k == 0 else 1 - g, c), :]
-        return remote(here, here, w_send.at[2 + k], w_recv.at[2 + k], "cfg", 1 - c)
+            w_ref.at[w_rows(g, c, k), there], w_peer.at[w_rows(g, c, k), :],
+            w_send.at[0, k], w_recv.at[0, k], "fsdp", 1 - f)
+
+    def w_y(k):
+        here = w_peer.at[w_rows(g, c, k), :]
+        return remote(here, here, w_send.at[1, k], w_recv.at[1, k], "groups", 1 - g)
+
+    def w_core(hop, k):
+        here = w_peer.at[w_rows(g if hop == 0 else 1 - g, c, k), :]
+        return remote(here, here, w_send.at[2 + hop, k], w_recv.at[2 + hop, k], "cfg", 1 - c)
 
     @pl.when(is_edge)
     def _():
@@ -234,7 +234,6 @@
         def _(t):
             send_own(t)
 
-    w_x().start()
     q_in = pltpu.make_async_copy(q_hbm.at[0], q, local_sem.at[0])
     fresh_in = pltpu.make_async_copy(fresh_ref.at[0], kv.at[:, span(z), :], local_sem.at[1])
     hidden_in = pltpu.make_async_copy(hidden_ref.at[0], hidden, local_sem.at[2])
@@ -250,7 +249,9 @@
     def _():
         stale_in.start()
 
+    gates_in = pltpu.make_async_copy(gate_ref, gates, local_sem.at[5])
     hidden_in.start()
+    gates_in.start()
     w_in.start()
     q_in.wait()
     fresh_in.wait()
@@ -260,8 +261,12 @@
         stale_in.wait()
 
     take(1, 0)
-    x_step = jnp.where(is_edge, 2, 4)
-    y_step = jnp.where(is_edge, near, heads - 1)
+    early = heads - 2
+    step = 512
+
+    def project(begin, end, part):
+        mine = jnp.dot(att[:, begin:end], w_own[begin:end, part], preferred_element_type=jnp.float32)
+        return mine + jnp.dot(att_peer[:, begin:end], w_peer[begin:end, part], preferred_element_type=jnp.float32)
 
     @pl.loop(0, heads)
     def _(t):
@@ -273,19 +278,39 @@
         def _():
             take(1, t + 1)
 
+        @pl.when(t < 4)
+        def _():
+            w_x(t).start()
+
+        @pl.when((t >= 2) & (t < 6))
+        def _():
+            w_x(t - 2).wait_recv()
+            w_y(t - 2).start()
+            w_core(0, t - 2).start()
+
+        @pl.when((t >= 4) & (t < 8))
+        def _():
+            w_y(t - 4).wait_recv()
+            w_core(1, t - 4).start()
+
+        @pl.when(t == heads - 1)
+        def _():
+            for k in range(4):
+                w_core(0, k).wait_recv()
+                w_core(1, k).wait_recv()
+            w_in.wait()
+
+            @pl.loop(0, early)
+            def _(h):
+                att_copy(h).wait_recv()
+
+            @pl.loop(0, columns // step)
+            def _(n):
+                part = pl.ds(pl.multiple_of(n * step, step), step)
+                total[:, part] = project(0, early * HEAD, part)
+
         take(2, t)
         take(3, t)
-
-        @pl.when(t == x_step)
-        def _():
-            w_x().wait_recv()
-            w_y().start()
-            w_core(0).start()
-
-        @pl.when(t == y_step)
-        def _():
-            w_y().wait_recv()
-            w_core(1).start()
 
         @pl.when(inner & (t >= near))
         def _():
@@ -310,30 +335,27 @@
 
         att_copy(t).start()
 
-    w_in.wait()
     hidden_in.wait()
-    w_core(0).wait_recv()
-    w_core(1).wait_recv()
-
-    @pl.loop(0, heads)
+    gates_in.wait()
+
+    @pl.loop(early, heads)
     def _(t):
         att_copy(t).wait_recv()
-
-    step = 512
 
     @pl.loop(0, columns // step)
     def _(n):
         part = pl.ds(pl.multiple_of(n * step, step), step)
-        mine = jnp.dot(att[...], w_own[:, part], preferred_element_type=jnp.float32)
-        other = jnp.dot(att_peer[...], w_peer[:, part], preferred_element_type=jnp.float32)
-        projected = mine.astype(jnp.bfloat16).astype(jnp.float32) + other.astype(jnp.bfloat16).astype(jnp.float32)
-        moved = hidden[:, part].astype(jnp.float32) + gate_ref[:, part] * projected
+        projected = total[:, part] + project(early * HEAD, heads * HEAD, part)
+        gate = gates[pl.ds(when_ref[0], 1), part]
+        moved = hidden[:, part].astype(jnp.float32) + gate * projected
         out_ref[:, part] = moved.astype(jnp.bfloat16)
 
-    w_x().wait_send()
-    w_y().wait_send()
-    w_core(0).wait_send()
-    w_core(1).wait_send()
+    @pl.loop(0, 4)
+    def _(k):
+        w_x(k).wait_send()
+        w_y(k).wait_send()
+        w_core(0, k).wait_send()
+        w_core(1, k).wait_send()
 
     @pl.loop(0, heads)
     def _(t):
@@ -361,15 +383,14 @@
     heads = width // HEAD
     tokens = rows * lax.axis_size("patch")
     columns = hidden_states.shape[2]
-    far_heads = (2 * heads) // 5
-    gate_row = lax.dynamic_index_in_dim(gate_table, timestep[0], 0, keepdims=True)
+    far_heads = heads // 2
     bf16 = jnp.bfloat16
     hbm = pl.BlockSpec(memory_space=pl.ANY)
     dma = pltpu.SemaphoreType.DMA
     out = pl.pallas_call(
         functools.partial(fused_kernel, far_heads),
         out_shape=jax.ShapeDtypeStruct((rows, columns), bf16),
-        in_specs=[hbm] * 5 + [pl.BlockSpec(memory_space=pltpu.VMEM)],
+        in_specs=[hbm] * 6 + [pl.BlockSpec(memory_space=pltpu.SMEM)],
         out_specs=pl.BlockSpec(memory_space=pltpu.VMEM),
         scratch_shapes=[
             pltpu.VMEM((2, tokens, width), bf16),
@@ -382,7 +403,9 @@
             pltpu.VMEM((width, columns), bf16),
             pltpu.VMEM((width, columns), bf16),
             pltpu.VMEM((rows, columns), bf16),
-            dma((5,)),
+            pltpu.VMEM(gate_table.shape, jnp.float32),
+            pltpu.VMEM((rows, columns), jnp.float32),
+            dma((6,)),
             dma((2, 3, heads)),
             dma((4, heads)),
             dma((2, far_heads)),
@@ -391,12 +414,12 @@
             dma((far_heads,)),
             dma((heads,)),
             dma((heads,)),
-            dma((4,)),
-            dma((4,)),
+            dma((4, 4)),
+            dma((4, 4)),
         ],
         compiler_params=pltpu.CompilerParams(
             collective_id=0, has_side_effects=True, vmem_limit_bytes=56 << 20),
-    )(hidden_states, queries, fresh_kv, stale_kv, out_weight, gate_row)
+    )(hidden_states, queries, fresh_kv, stale_kv, out_weight, gate_table, timestep)
     return out[None]
 
 

time: 119 us -> 113 us (0.950)
  Pallas kernels: 114 us -> 109 us
    pallas_call x1, Pallas kernels: 114 us -> 109 us  [fused_local(): pl.pallas_call(functools.partial(fused_kernel, far_heads), out_shape=jax....]
    unnamed x3 -> x1, local copies, waits for them, and re-layouts: 3.3 us -> 2.94 us
where the time goes in v2:
time: 113 us
  Pallas kernels  109 us (96%)
  local copies, waits for them, and re-layouts  2.94 us (3%)
    pallas_call x1, Pallas kernels, fused_local(): pl.pallas_call(functools.partial(fused_kernel, far_heads), out_shape=jax....  109 us
    unnamed x1, local copies, waits for them, and re-layouts  2.94 us

profile of v2, /device:TPU:0, one launch (start us, length us, event | category | flops | bytes accessed | tf_op | source)
XLA Modules:
  0.0 112.8 jit_solution(9733214652812262062)
XLA Ops:
  0.7 109.2 %shard_map.73 = bf16[384,2560]{1,0:T(8,128)(2,1)} custom-call(bf16[1,384,2560]{2,1,0:T(8,128)(2,1)} %hidden_ref.1, bf16[1,384,1280]{2,1,0:T(8,128)(2,1)} %q_hbm.1, bf16[1,2,384,1280]{3,2,1,0:T(8,128)(2,1)} %fresh_ref.1, bf16[1,2,384,1280]{3,2,1,0:T(8,128)(2,1)} %stale_ref.1, bf16[1280,5120]{1,0:T(8,128)(2,1)} %w_ref.1, f32[50,2560]{1,0:T(8,128)} %gate_ref.1, ...), custom_call_target="tpu_custom_call" | custom-call | tf_op jit(solution)/shard_map/pallas_call | solution.py:390
  109.8 2.9 %copy.10 = bf16[1,384,2560]{2,1,0:T(8,128)(2,1)} copy(bf16[1,384,2560]{2,1,0:T(8,128)(2,1)} %bitcast.1) | data formatting | bytes 3932160

commit v3 on v2

--- a/solution.py
+++ b/solution.py
@@ -57,17 +57,18 @@
 
 
 MESH = pl.DeviceIdType.MESH
-LEAD = 3
-
-
-def attend_head(q_ref, q_cols, k_ref, v_ref, kv_cols, o_ref, o_cols):
+LEAD = 2
+TILE = 128
+AHEAD = 2
+
+
+def attend_head(q_ref, q_cols, k_ref, v_ref, kv_cols, o_ref, o_cols, done):
     rows = q_ref.shape[0]
-    tile = 128
     factor = HEAD ** (-0.5) * math.log2(math.e)
     keys = k_ref[:, kv_cols]
     values = v_ref[:, kv_cols]
-    for start in range(0, rows, tile):
-        part = slice(start, start + tile)
+    for r in range(rows // TILE):
+        part = slice(r * TILE, (r + 1) * TILE)
         scores = lax.dot_general(
             q_ref[part, q_cols], keys, (((1,), (1,)), ((), ())), preferred_element_type=jnp.float32
         )
@@ -76,6 +77,7 @@
         total = jnp.sum(weights, axis=-1, keepdims=True)
         summed = jnp.dot(weights.astype(jnp.bfloat16), values, preferred_element_type=jnp.float32)
         o_ref[part, o_cols] = (summed / total).astype(jnp.bfloat16)
+        done(r)
 
 
 def fused_kernel(
@@ -190,18 +192,24 @@
         here = helped_kv.at[:, span(edge), cols(i)]
         return remote(here, here, edge_send.at[1, i], edge_recv.at[1, i], "patch", edge_to)
 
-    def result_copy(i):
+    tiles = rows // TILE
+
+    def result_copy(i, r):
+        part = slice(r * TILE, (r + 1) * TILE)
         return remote(
-            helped_out.at[:, cols(i)], att.at[:, cols(near + i)],
-            res_send.at[i], res_recv.at[i], "patch", edge_to)
-
-    def att_copy(t):
-        return remote(att.at[:, cols(t)], att_peer.at[:, cols(t)], att_send.at[t], att_recv.at[t], "fsdp", 1 - f)
+            helped_out.at[part, cols(i)], att.at[part, cols(near + i)],
+            res_send.at[i, r], res_recv.at[i, r], "patch", edge_to)
+
+    def att_copy(t, r):
+        part = slice(r * TILE, (r + 1) * TILE)
+        return remote(
+            att.at[part, cols(t)], att_peer.at[part, cols(t)],
+            att_send.at[t, r], att_recv.at[t, r], "fsdp", 1 - f)
 
     piece = w_peer.shape[0] // 16
 
     def w_rows(gi, ci, k):
-        return pl.ds(pl.multiple_of(((gi * 2 + ci) * 4 + k) * piece, piece), piece)
+        return pl.ds(pl.multiple_of((k * 4 + gi * 2 + ci) * piece, piece), piece)
 
     def w_x(k):
         there = pl.ds(pl.multiple_of((1 - f) * columns, columns), columns)
@@ -216,17 +224,6 @@
     def w_core(hop, k):
         here = w_peer.at[w_rows(g if hop == 0 else 1 - g, c, k), :]
         return remote(here, here, w_send.at[2 + hop, k], w_recv.at[2 + hop, k], "cfg", 1 - c)
-
-    @pl.when(is_edge)
-    def _():
-        @pl.loop(0, heads)
-        def _(t):
-            send_own(t)
-
-            @pl.when(t >= near)
-            def _():
-                edge_q(t - near).start()
-                edge_kv(t - near).start()
 
     @pl.when(inner)
     def _():
@@ -260,13 +257,60 @@
     def _():
         stale_in.wait()
 
+    def w_tick(u):
+        @pl.when(u < 4)
+        def _():
+            w_x(u).start()
+
+        @pl.when((u >= 2) & (u < 6))
+        def _():
+            w_x(u - 2).wait_recv()
+            w_y(u - 2).start()
+            w_core(0, u - 2).start()
+
+        @pl.when((u >= 4) & (u < 8))
+        def _():
+            w_y(u - 4).wait_recv()
+            w_core(1, u - 4).start()
+
+    @pl.when(is_edge)
+    def _():
+        @pl.loop(0, heads)
+        def _(m):
+            send_own(m)
+
+            @pl.when(m % 2 == 0)
+            def _():
+                w_tick(m // 2)
+
+            for way in (0, 1):
+                @pl.when((m >= AHEAD) & does_send(way, 0, m))
+                def _():
+                    kv_copy(way, 0, m - AHEAD).wait_send()
+
     take(1, 0)
     early = heads - 2
+    half = early // 2
     step = 512
 
-    def project(begin, end, part):
-        mine = jnp.dot(att[:, begin:end], w_own[begin:end, part], preferred_element_type=jnp.float32)
-        return mine + jnp.dot(att_peer[:, begin:end], w_peer[begin:end, part], preferred_element_type=jnp.float32)
+    def w_taken(k):
+        w_core(0, k).wait_recv()
+        w_core(1, k).wait_recv()
+
+    def att_taken(begin, end):
+        @pl.loop(begin, end)
+        def _(h):
+            for r in range(tiles):
+                att_copy(h, r).wait_recv()
+
+    def add_up(left, right, begin, end, first):
+        deep = slice(begin * HEAD, end * HEAD)
+
+        @pl.loop(0, columns // step)
+        def _(n):
+            part = pl.ds(pl.multiple_of(n * step, step), step)
+            term = jnp.dot(left[:, deep], right[deep, part], preferred_element_type=jnp.float32)
+            total[:, part] = term if first else total[:, part] + term
 
     @pl.loop(0, heads)
     def _(t):
@@ -278,36 +322,12 @@
         def _():
             take(1, t + 1)
 
-        @pl.when(t < 4)
-        def _():
-            w_x(t).start()
-
-        @pl.when((t >= 2) & (t < 6))
-        def _():
-            w_x(t - 2).wait_recv()
-            w_y(t - 2).start()
-            w_core(0, t - 2).start()
-
-        @pl.when((t >= 4) & (t < 8))
-        def _():
-            w_y(t - 4).wait_recv()
-            w_core(1, t - 4).start()
-
-        @pl.when(t == heads - 1)
-        def _():
-            for k in range(4):
-                w_core(0, k).wait_recv()
-                w_core(1, k).wait_recv()
-            w_in.wait()
-
-            @pl.loop(0, early)
-            def _(h):
-                att_copy(h).wait_recv()
-
-            @pl.loop(0, columns // step)
-            def _(n):
-                part = pl.ds(pl.multiple_of(n * step, step), step)
-                total[:, part] = project(0, early * HEAD, part)
+        w_tick(jnp.where(is_edge, t + heads // 2, t))
+
+        @pl.when(is_edge & (t < far_heads))
+        def _():
+            edge_q(t).start()
+            edge_kv(t).start()
 
         take(2, t)
         take(3, t)
@@ -322,30 +342,54 @@
                 def _():
                     part = slice(p * rows, (p + 1) * rows)
                     helped_kv[:, part, cols(i)] = kv[:, part, cols(t)]
-            attend_head(helped_q, cols(i), helped_kv.at[0], helped_kv.at[1], cols(i), helped_out, cols(i))
-            result_copy(i).start()
+            attend_head(helped_q, cols(i), helped_kv.at[0], helped_kv.at[1], cols(i), helped_out, cols(i),
+                        lambda r: result_copy(i, r).start())
+
+        @pl.when(t == half)
+        def _():
+            w_in.wait()
+            add_up(att, w_own, 0, half, True)
+
+        @pl.when(t == heads - 4)
+        def _():
+            w_taken(0)
+            w_taken(1)
+            att_taken(0, half)
+            add_up(att_peer, w_peer, 0, half, False)
+
+        @pl.when(t == heads - 2)
+        def _():
+            add_up(att, w_own, half, early, False)
+
+        @pl.when(t == heads - 1)
+        def _():
+            w_taken(2)
+            w_taken(3)
+            att_taken(half, early)
+            add_up(att_peer, w_peer, half, early, False)
 
         @pl.when(inner | (t < near))
         def _():
-            attend_head(q, cols(t), kv.at[0], kv.at[1], cols(t), att, cols(t))
+            attend_head(q, cols(t), kv.at[0], kv.at[1], cols(t), att, cols(t),
+                        lambda r: att_copy(t, r).start())
 
         @pl.when(is_edge & (t >= near))
         def _():
-            result_copy(t - near).wait_recv()
-
-        att_copy(t).start()
+            for r in range(tiles):
+                result_copy(t - near, r).wait_recv()
+                att_copy(t, r).start()
 
     hidden_in.wait()
     gates_in.wait()
-
-    @pl.loop(early, heads)
-    def _(t):
-        att_copy(t).wait_recv()
+    add_up(att, w_own, early, heads, False)
+
+    att_taken(early, heads)
 
     @pl.loop(0, columns // step)
     def _(n):
         part = pl.ds(pl.multiple_of(n * step, step), step)
-        projected = total[:, part] + project(early * HEAD, heads * HEAD, part)
+        projected = total[:, part] + jnp.dot(
+            att_peer[:, early * HEAD:], w_peer[early * HEAD:, part], preferred_element_type=jnp.float32)
         gate = gates[pl.ds(when_ref[0], 1), part]
         moved = hidden[:, part].astype(jnp.float32) + gate * projected
         out_ref[:, part] = moved.astype(jnp.bfloat16)
@@ -359,10 +403,12 @@
 
     @pl.loop(0, heads)
     def _(t):
-        att_copy(t).wait_send()
+        for r in range(tiles):
+            att_copy(t, r).wait_send()
         for way in (0, 1):
             for hop in (0, 1, 2):
-                @pl.when(does_send(way, hop, t))
+                waited = is_edge & (t < heads - AHEAD) if hop == 0 else False
+                @pl.when(does_send(way, hop, t) & jnp.logical_not(waited))
                 def _():
                     kv_copy(way, hop, t).wait_send()
 
@@ -375,7 +421,8 @@
 
         @pl.when(inner)
         def _():
-            result_copy(i).wait_send()
+            for r in range(tiles):
+                result_copy(i, r).wait_send()
 
 
 def fused_local(hidden_states, queries, fresh_kv, stale_kv, out_weight, gate_table, timestep):
@@ -410,10 +457,10 @@
             dma((4, heads)),
             dma((2, far_heads)),
             dma((2, far_heads)),
-            dma((far_heads,)),
-            dma((far_heads,)),
-            dma((heads,)),
-            dma((heads,)),
+            dma((far_heads, rows // TILE)),
+            dma((far_heads, rows // TILE)),
+            dma((heads, rows // TILE)),
+            dma((heads, rows // TILE)),
             dma((4, 4)),
             dma((4, 4)),
         ],

time: 113 us -> 111 us (0.982)
  Pallas kernels: 109 us -> 107 us
    pallas_call x1, Pallas kernels: 109 us -> 107 us  [fused_local(): pl.pallas_call(functools.partial(fused_kernel, far_heads), out_shape=jax....]
where the time goes in v3:
time: 111 us; the launch traced here: 110 us
  Pallas kernels  107 us (96%)
  local copies, waits for them, and re-layouts  2.94 us (3%)
    pallas_call x1, Pallas kernels, fused_local(): pl.pallas_call(functools.partial(fused_kernel, far_heads), out_shape=jax....  107 us
    unnamed x1, local copies, waits for them, and re-layouts  2.94 us

profile of v3, /device:TPU:0, one launch (start us, length us, event | category | flops | bytes accessed | tf_op | source)
XLA Modules:
  0.0 110.5 jit_solution(1193713087461800538)
XLA Ops:
  0.7 106.9 %shard_map.73 = bf16[384,2560]{1,0:T(8,128)(2,1)} custom-call(bf16[1,384,2560]{2,1,0:T(8,128)(2,1)} %hidden_ref.1, bf16[1,384,1280]{2,1,0:T(8,128)(2,1)} %q_hbm.1, bf16[1,2,384,1280]{3,2,1,0:T(8,128)(2,1)} %fresh_ref.1, bf16[1,2,384,1280]{3,2,1,0:T(8,128)(2,1)} %stale_ref.1, bf16[1280,5120]{1,0:T(8,128)(2,1)} %w_ref.1, f32[50,2560]{1,0:T(8,128)} %gate_ref.1, ...), custom_call_target="tpu_custom_call" | custom-call | tf_op jit(solution)/shard_map/pallas_call | solution.py:437
  107.5 2.9 %copy.10 = bf16[1,384,2560]{2,1,0:T(8,128)(2,1)} copy(bf16[1,384,2560]{2,1,0:T(8,128)(2,1)} %bitcast.1) | data formatting | bytes 3932160
